TPU v7x, 256 devices: a whole 4x4x8 slice. The times are simulated.
256 devices in a mesh: clu: 64 (over z, y, core), grp: 4 (over x).
Axes of the slice: x: 4, y: 4, z: 8, core: 2. Of those that a mesh axis runs over, the one named last changes fastest.
Arguments:
- embeddings: bfloat16 [131072, 768], P(('clu', 'grp')), may hold values from -6 to 6
- cluster_of: int32 [131072], P(('clu', 'grp')), may hold values from 0 to 127, as said below
- new_rows: bfloat16 [4096, 768], P(('clu', 'grp')), may hold values from -6 to 6
- centroids: bfloat16 [65536, 768], P(('clu', 'grp')), may hold values from -6 to 6
Outputs:
- dup_score: float32 [131072], P(('clu', 'grp'))
- centroid_score: float32 [4096], P(('clu', 'grp'))
Inputs may be any that keep to these rules, and one draw needn't show every extreme that they name: `cluster_of`: cluster k is owned by owner k mod 64; among the 512 rows of one device, at most 16 rows belong to the clusters of one owner, and in every such block some owner has exactly 16.
All inputs are finite; a program needn't handle non-finite values.
Results may differ from a plain program's by a relative error of at most 0.0015.
Values may be sent and summed in bfloat16 or wider, within the bound.
No kernel may reach another device: no remote copies, remote signals or barrier semaphores. Data moves between devices by JAX's collectives and lax.ppermute only.
A program may use at most 64 MiB of HBM per device.

v0:
```python
import functools

import jax
import jax.numpy as jnp
from jax import lax
from jax.experimental import pallas as pl
from jax.experimental.pallas import tpu as pltpu
from jax.sharding import Mesh
from jax.sharding import PartitionSpec as P

EPS = 1e-06
OWN = ("z", "y", "xh")
ALL = ("z", "y", "c", "xh", "xl")
SWAP = [(0, 1), (1, 0)]
BF16 = jnp.bfloat16
F32 = jnp.float32
NOTE = 8
INFO = 16
VMEM_LIMIT = 48 * 1024 * 1024


def unit_rows(rows):
    wide = rows.astype(F32)
    total = jnp.sum(wide * wide, axis=-1, keepdims=True)
    return (wide * lax.rsqrt(total + EPS)).astype(BF16)


def dot_t(left, right):
    return lax.dot_general(left, right, (((1,), (1,)), ((), ())), preferred_element_type=F32)


def params(**kwargs):
    return pltpu.CompilerParams(vmem_limit_bytes=VMEM_LIMIT, **kwargs)


def cost(flops, moved):
    return pl.CostEstimate(flops=flops, bytes_accessed=moved, transcendentals=0)


def column_to_grid(column, owners, cap):
    wide = jnp.broadcast_to(column.reshape(owners, cap, 1), (owners, cap, 128))
    sub = lax.broadcasted_iota(jnp.int32, (owners, cap, 128), 1)
    lane = lax.broadcasted_iota(jnp.int32, (owners, cap, 128), 2)
    return jnp.sum(jnp.where(sub == lane, wide, 0.0), axis=1)[:, :cap]


def pack_kernel(cap, emb_ref, clu_ref, send_ref, place_ref):
    owners = send_ref.shape[0]
    rows, width = emb_ref.shape
    cluster = clu_ref[...]
    target = lax.rem(cluster, owners)
    owner_of = lax.broadcasted_iota(jnp.int32, (owners, rows), 0)
    hot = target == owner_of
    first = lax.broadcasted_iota(jnp.int32, (rows, rows), 0)
    second = lax.broadcasted_iota(jnp.int32, (rows, rows), 1)
    before = jnp.where(first < second, 1.0, 0.0).astype(BF16)
    ahead = jnp.dot(
        jnp.where(hot, 1.0, 0.0).astype(BF16), before, preferred_element_type=F32
    )
    rank = jnp.sum(jnp.where(hot, ahead, 0.0), axis=0, keepdims=True).astype(jnp.int32)
    place_ref[0:1, :] = target
    place_ref[1:2, :] = rank
    units = unit_rows(emb_ref[...])
    slot = target * cap + rank
    row_of = lax.broadcasted_iota(jnp.int32, (owners * cap, rows), 0)
    pick = jnp.where(row_of == slot, 1.0, 0.0).astype(BF16)
    send = jnp.dot(pick, units, preferred_element_type=F32).astype(BF16)
    for k in range(width // 128):
        piece = send[:, k * 128 : (k + 1) * 128].reshape(owners, cap, 128)
        send_ref[:, k * cap : (k + 1) * cap, :] = piece
    code = jnp.where(hot, cluster.astype(F32) + 1.0, 0.0)
    lane = lax.broadcasted_iota(jnp.int32, (owners, 128), 1)
    ids = jnp.full((owners, 128), -1.0, F32)
    for k in range(cap):
        held = jnp.sum(jnp.where(rank == k, code, 0.0), axis=1, keepdims=True)
        ids = jnp.where(lane == k, held - 1.0, ids)
    notes = jnp.broadcast_to(ids.reshape(owners, 1, 128), (owners, NOTE, 128))
    send_ref[:, width // 128 * cap :, :] = notes.astype(BF16)


def pack(emb, cluster, owners, cap):
    rows, width = emb.shape
    return pl.pallas_call(
        functools.partial(pack_kernel, cap),
        out_shape=(
            jax.ShapeDtypeStruct((owners, width // 128 * cap + NOTE, 128), BF16),
            jax.ShapeDtypeStruct((2, rows), jnp.int32),
        ),
        compiler_params=params(),
        cost_estimate=cost(2 * owners * cap * rows * width, 3 * rows * width * 2),
    )(emb, cluster.reshape(1, rows))


def tie(array, *others):
    return pl.pallas_call(
        lambda *refs: None,
        in_specs=[pl.BlockSpec(memory_space=pl.ANY)] * (1 + len(others)),
        out_specs=pl.BlockSpec(memory_space=pl.ANY),
        out_shape=jax.ShapeDtypeStruct(array.shape, array.dtype),
        input_output_aliases={0: 0},
    )(array, *others)


def unit_kernel(in_ref, out_ref):
    out_ref[...] = unit_rows(in_ref[...])


def unit(rows):
    return pl.pallas_call(
        unit_kernel,
        out_shape=jax.ShapeDtypeStruct(rows.shape, BF16),
        compiler_params=params(),
        cost_estimate=cost(4 * rows.size, 4 * rows.size),
    )(rows)


def cent_kernel(owners, cap, steps_y, steps_z, where_ref, mine_ref, other_ref, *refs):
    cent_ref, out_refs = refs[0], refs[-2:]
    at_z, at_y, at_xh = where_ref[0], where_ref[1], where_ref[2]
    for new_ref, out_ref in zip((mine_ref, other_ref), out_refs):
        new_unit = unit_rows(new_ref[...])
        best = jnp.max(dot_t(new_unit, cent_ref[...]), axis=1, keepdims=True)
        grid = column_to_grid(best, new_unit.shape[0] // cap, cap)
        out_ref[...] = jnp.full((owners, cap), -3.0, F32)
        k = 0
        for dy in steps_y:
            for dz in steps_z:
                source = lax.rem(at_z + dz, 8) * 4 + lax.rem(at_y + 4 + dy, 4)
                out_ref[pl.ds(source * 2 + at_xh, 1), :] = grid[k : k + 1, :]
                k += 1


def cent_best(where, mine, other, cents, owners, cap, steps_y, steps_z):
    rows, width = mine.shape
    count = cents.shape[0]
    vmem = pl.BlockSpec(memory_space=pltpu.VMEM)
    return pl.pallas_call(
        functools.partial(cent_kernel, owners, cap, steps_y, steps_z),
        in_specs=[pl.BlockSpec(memory_space=pltpu.SMEM)] + [vmem] * 3,
        out_shape=(jax.ShapeDtypeStruct((owners, cap), F32),) * 2,
        compiler_params=params(),
        cost_estimate=cost(4 * rows * count * width, (2 * rows + count) * width * 2),
    )(where, mine, other, cents)


def block_rows(block, cap):
    blocks, deep, _ = block.shape
    pieces = (deep - NOTE) // cap
    return jnp.concatenate(
        [block[:, k * cap : (k + 1) * cap, :].reshape(blocks * cap, 128) for k in range(pieces)],
        axis=1,
    )


def block_ids(block, cap):
    blocks, deep, _ = block.shape
    notes = block[:, deep - NOTE :, :].astype(F32)[:, 0:1, :]
    sub = lax.broadcasted_iota(jnp.int32, (blocks, cap, 128), 1)
    lane = lax.broadcasted_iota(jnp.int32, (blocks, cap, 128), 2)
    spread = jnp.where(sub == lane, jnp.broadcast_to(notes, (blocks, cap, 128)), 0.0)
    return spread.reshape(blocks * cap, 128)


def dup_kernel(tiles, cap, count, with_self, first, last, own_ref, *refs):
    col_refs, refs = refs[:count], refs[count:]
    if not first:
        old_ref, refs = refs[0], refs[1:]
    out_ref, own, own_ids = refs[:3]
    acc = refs[3] if last else out_ref
    step = pl.program_id(0)
    rows = own.shape[0]

    @pl.when(step == 0)
    def _():
        acc[...] = jnp.full(acc.shape, -1.0, F32) if first else old_ref[...]
        own[...] = block_rows(own_ref[...], cap)
        own_ids[...] = jnp.sum(block_ids(own_ref[...], cap), axis=1, keepdims=True)

    for k, col_ref in enumerate(col_refs):
        block = col_ref[...]
        other = block_rows(block, cap)
        tile = other.shape[0]
        spread = block_ids(block, cap).astype(BF16)
        col_ids = dot_t(jnp.full((8, 128), 1.0, BF16), spread)[0:1, :]
        match = own_ids[...] == jnp.where(col_ids < 0, -2.0, col_ids)
        if with_self and k == 0:
            row = lax.broadcasted_iota(jnp.int32, (rows, tile), 0)
            col = lax.broadcasted_iota(jnp.int32, (rows, tile), 1) + step * tile
            match = match & (row != col)
        kept = jnp.where(match, dot_t(own[...], other), -1.0)
        best = acc[...]
        for j in range(tile // 128):
            best = jnp.maximum(best, kept[:, j * 128 : (j + 1) * 128])
        acc[...] = best

    if last:

        @pl.when(step == tiles - 1)
        def _():
            top = jnp.max(acc[...], axis=1, keepdims=True)
            out_ref[...] = column_to_grid(top, own_ref.shape[0], cap)


def dup_best(own, cols, cap, with_self=False, old=None, last=False):
    owners, deep, _ = own.shape
    rows, width = owners * cap, (deep - NOTE) // cap * 128
    each = 16
    tiles = owners // each
    whole = lambda array: pl.BlockSpec(array.shape, lambda j: (0,) * len(array.shape))
    held = jax.ShapeDtypeStruct((rows, 128), F32)
    out_shape = jax.ShapeDtypeStruct((owners, cap), F32) if last else held
    more = [] if old is None else [old]
    return pl.pallas_call(
        functools.partial(dup_kernel, tiles, cap, len(cols), with_self, old is None, last),
        grid=(tiles,),
        in_specs=[whole(own)]
        + [pl.BlockSpec((each, deep, 128), lambda j: (j, 0, 0))] * len(cols)
        + [whole(a) for a in more],
        out_specs=whole(out_shape),
        out_shape=out_shape,
        scratch_shapes=[pltpu.VMEM((rows, width), BF16), pltpu.VMEM((rows, 1), F32)]
        + ([pltpu.VMEM((rows, 128), F32)] if last else []),
        compiler_params=params(),
        cost_estimate=cost(
            2 * rows * rows * len(cols) * width, (1 + len(cols)) * rows * width * 2
        ),
    )(own, *cols, *more)


def split_kernel(cap, room, where_ref, own_ref, keep_ref, give_ref, place_ref):
    owners, deep, _ = own_ref.shape
    block = own_ref[...]
    rows = block_rows(block, cap)
    slots, width = rows.shape
    ids = block[:, deep - NOTE :, :].astype(F32)[:, 0, :]
    side = jnp.where(ids >= owners, 1.0, 0.0)
    here = where_ref[3].astype(F32)
    upper = lax.broadcasted_iota(jnp.int32, (128, 128), 0) < lax.broadcasted_iota(
        jnp.int32, (128, 128), 1
    )
    lower = lax.broadcasted_iota(jnp.int32, (owners, owners), 1) < lax.broadcasted_iota(
        jnp.int32, (owners, owners), 0
    )
    upper = jnp.where(upper, 1.0, 0.0).astype(BF16)
    lower = jnp.where(lower, 1.0, 0.0).astype(BF16)
    sub = lax.broadcasted_iota(jnp.int32, (owners, cap, 128), 1)
    lane = lax.broadcasted_iota(jnp.int32, (owners, cap, 128), 2)
    ones = jnp.full((8, 128), 1.0, BF16)
    list_row = lax.broadcasted_iota(jnp.int32, (room, slots), 0).astype(F32)

    def as_row(grid):
        wide = jnp.broadcast_to(grid.reshape(owners, 1, 128), (owners, cap, 128))
        spread = jnp.where(sub == lane, wide, 0.0).reshape(slots, 128)
        return dot_t(ones, spread.astype(BF16))[0:1, :]

    members = []
    for part, out_ref in enumerate((keep_ref, give_ref)):
        chosen = (ids >= 0) & ((side == here) if part == 0 else (side != here))
        mask = jnp.where(chosen, 1.0, 0.0)
        packed = mask.astype(BF16)
        within = jnp.dot(packed, upper, preferred_element_type=F32)
        above = jnp.sum(jnp.dot(lower, packed, preferred_element_type=F32), axis=1, keepdims=True)
        after = jnp.where(chosen, within + above + 1.0, 0.0)
        high = jnp.floor(after * (1.0 / 32.0))
        rank = 32.0 * as_row(high) + as_row(after - 32.0 * high) - 1.0
        pick = jnp.where(list_row == rank, 1.0, 0.0).astype(BF16)
        out_ref[:room, :] = jnp.dot(pick, rows, preferred_element_type=F32).astype(BF16)
        place_ref[part * owners : (part + 1) * owners, :] = after - 1.0
        members.append(jnp.sum(jnp.sum(mask, axis=1, keepdims=True), axis=0, keepdims=True))
    over = jnp.where((members[0] > room) | (members[1] > room), 1.0, 0.0)
    spot = lax.broadcasted_iota(jnp.int32, (INFO, width), 1)
    for count, out_ref in zip(members, (keep_ref, give_ref)):
        high = jnp.floor(count * (1.0 / 32.0))
        info = jnp.where(spot == 0, high, jnp.where(spot == 1, count - 32.0 * high, over))
        out_ref[room:, :] = info.astype(BF16)


def split(where, own, cap, room):
    owners, deep, _ = own.shape
    width = (deep - NOTE) // cap * 128
    rows = owners * cap
    vmem = pl.BlockSpec(memory_space=pltpu.VMEM)
    return pl.pallas_call(
        functools.partial(split_kernel, cap, room),
        in_specs=[pl.BlockSpec(memory_space=pltpu.SMEM), vmem],
        out_shape=(
            jax.ShapeDtypeStruct((room + INFO, width), BF16),
            jax.ShapeDtypeStruct((room + INFO, width), BF16),
            jax.ShapeDtypeStruct((2 * owners, 128), F32),
        ),
        compiler_params=params(),
        cost_estimate=cost(4 * rows * room * width, 3 * rows * width),
    )(where, own)


def list_kernel(room, *refs):
    list_refs, (keep_ref, came_ref) = refs[:4], refs[4:]
    over = jnp.zeros((1, 1), F32)
    counts = []
    for ref in list_refs:
        info = ref[room:, :128].astype(F32)
        counts.append(32.0 * info[0:1, 0:1] + info[0:1, 1:2])
        over = jnp.maximum(over, info[0:1, 2:3])
    other = lax.broadcasted_iota(jnp.int32, (room, room), 0)
    mine = lax.broadcasted_iota(jnp.int32, (room, room), 1)
    position = lax.broadcasted_iota(jnp.int32, (room, 1), 0).astype(F32)
    for k, out_ref in ((0, keep_ref), (1, came_ref)):
        own = list_refs[k][:room, :]
        best = jnp.full((1, room), -1.0, F32)
        for j, ref in enumerate(list_refs):
            scores = dot_t(ref[:room, :], own)
            use = position < counts[j]
            if j == k:
                use = use & (other != mine)
            best = jnp.maximum(best, jnp.max(jnp.where(use, scores, -1.0), axis=0, keepdims=True))
        out_ref[:, :room] = best
        out_ref[:, room:] = jnp.broadcast_to(over, (1, 128))


def list_best(lists, room):
    width = lists[0].shape[1]
    return pl.pallas_call(
        functools.partial(list_kernel, room),
        out_shape=(jax.ShapeDtypeStruct((1, room + 128), F32),) * 2,
        compiler_params=params(),
        cost_estimate=cost(16 * room * room * width, 8 * room * width),
    )(*lists)


def merge_kernel(owners, cap, room, kept_ref, back_ref, place_ref, mine_ref, other_ref, out_ref):
    slots = owners * cap
    sub = lax.broadcasted_iota(jnp.int32, (owners, cap, 128), 1)
    lane = lax.broadcasted_iota(jnp.int32, (owners, cap, 128), 2)
    spot = lax.broadcasted_iota(jnp.int32, (slots, room), 1).astype(F32)
    total = jnp.zeros((slots, 1), F32)
    for part, ref in enumerate((kept_ref, back_ref)):
        grid = place_ref[part * owners : (part + 1) * owners, :]
        wide = jnp.broadcast_to(grid.reshape(owners, 1, 128), (owners, cap, 128))
        spread = jnp.where(sub == lane, wide, 0.0).reshape(slots, 128)
        place = jnp.sum(spread, axis=1, keepdims=True)
        found = jnp.where(spot == place, ref[:, :room], 0.0)
        total = total + jnp.sum(found, axis=1, keepdims=True)
    out_ref[:, :cap] = column_to_grid(total, owners, cap)
    out_ref[:, cap : 2 * cap] = jnp.maximum(mine_ref[...], other_ref[...])
    out_ref[:, 2 * cap :] = jnp.broadcast_to(kept_ref[:, room : room + cap], (owners, cap))


def merge(kept, back, place, mine, other, room):
    owners, cap = mine.shape
    return pl.pallas_call(
        functools.partial(merge_kernel, owners, cap, room),
        out_shape=jax.ShapeDtypeStruct((owners, 3 * cap), F32),
        compiler_params=params(),
    )(kept, back, place, mine, other)


def unpack_kernel(owners, cap, back_ref, place_ref, dup_ref, *more_refs):
    back = back_ref[...]
    target = place_ref[0:1, :]
    rank = place_ref[1:2, :]
    rows = target.shape[1]
    found = jnp.full((owners, rows), -2.0, F32)
    for k in range(cap):
        found = jnp.where(rank == k, back[:, k : k + 1], found)
    owner_of = lax.broadcasted_iota(jnp.int32, (owners, rows), 0)
    dup_ref[...] = jnp.max(jnp.where(target == owner_of, found, -2.0), axis=0, keepdims=True)
    for k, ref in enumerate(more_refs):
        ref[...] = jnp.max(back[:, (k + 1) * cap : (k + 2) * cap], axis=0, keepdims=True)


def unpack(back, place, owners, cap):
    rows = place.shape[1]
    more = back.shape[1] // cap - 1
    return pl.pallas_call(
        functools.partial(unpack_kernel, owners, cap),
        out_shape=[jax.ShapeDtypeStruct((1, rows), F32)]
        + [jax.ShapeDtypeStruct((1, cap), F32)] * more,
        compiler_params=params(),
    )(back, place)


def join_kernel(*refs):
    out_ref, at = refs[-1], 0
    for ref in refs[:-1]:
        out_ref[at : at + ref.shape[0], :] = ref[...]
        at += ref.shape[0]


def join(*blocks):
    rows, width = sum(b.shape[0] for b in blocks), blocks[0].shape[1]
    return pl.pallas_call(
        join_kernel,
        out_shape=jax.ShapeDtypeStruct((rows, width), blocks[0].dtype),
        compiler_params=params(),
        cost_estimate=cost(0, 4 * rows * width),
    )(*blocks)


def full_scores(own, place, cap):
    owners = own.shape[0]
    own_x = lax.ppermute(own, "xl", SWAP)
    own_c = lax.ppermute(own, "c", SWAP)
    own_cx = lax.ppermute(own_x, "c", SWAP)
    held = dup_best(own, [own, own_c], cap, with_self=True)
    best = dup_best(own, [own_x, own_cx], cap, old=held, last=True)
    back = lax.all_to_all(best, OWN, split_axis=0, concat_axis=0, tiled=True)
    return unpack(back, place, owners, cap)[0]


def moved(block, axis, size, by):
    return lax.ppermute(block, axis, [(i, (i - by) % size) for i in range(size)])


def shards(embeddings, cluster_of, new_rows, centroids):
    owners = lax.axis_size(OWN)
    rows, width = embeddings.shape
    cap = 2 * rows // owners
    room = 3 * rows // 4
    where = jnp.stack([lax.axis_index(a) for a in (*OWN, "xl")]).astype(jnp.int32)

    cents = lax.all_gather(unit(centroids), ("xh", "xl"), axis=0, tiled=True)
    line = join(new_rows, *(moved(new_rows, "z", 8, k) for k in (2, 4, 6)))
    steps_z = (0, 2, 4, 6, 1, 3, 5, 7)
    send, place = pack(embeddings, cluster_of, owners, cap)
    landed = lax.all_to_all(send, OWN, split_axis=0, concat_axis=0, tiled=True)
    own = tie(landed, cents, line)

    keep, give, spots = split(where, own, cap, room)
    came = lax.ppermute(give, "xl", SWAP)
    keep_c = lax.ppermute(keep, "c", SWAP)

    steps_y = (0, -1, 1, -2)
    line = join(line, moved(line, "z", 8, 1))
    left = lax.ppermute(line, "y", [(i, (i + 1) % 4) for i in range(4)])
    right = lax.ppermute(line, "y", [(i, (i + 3) % 4) for i in range(4)])
    far = lax.ppermute(line, "y", [(i, (i + 2) % 4) for i in range(4)])
    new = join(line, left, right, far)
    new_other = lax.ppermute(new, "c", SWAP)
    cent_mine, cent_theirs = cent_best(
        where, new, new_other, cents, owners, new_rows.shape[0], steps_y, steps_z
    )
    cent_back = lax.ppermute(cent_theirs, "c", SWAP)

    came_c = lax.ppermute(came, "c", SWAP)
    kept, guests = list_best([keep, came, keep_c, came_c], room)
    guests = lax.ppermute(guests, "xl", SWAP)
    both = merge(kept, guests, spots, cent_mine, cent_back, room)
    back = lax.all_to_all(both, OWN, split_axis=0, concat_axis=0, tiled=True)
    dup, cent_score, over = unpack(back, place, owners, cap)
    dup = lax.cond(
        over[0, 0] > 0.5,
        lambda held, spot, short: full_scores(held, spot, cap),
        lambda held, spot, short: short,
        own,
        place,
        dup,
    )
    return (dup.reshape(rows), cent_score.reshape(new_rows.shape[0]))


def solution(mesh):
    sizes = mesh.devices.shape
    owners, group = sizes
    halves = owners // 2
    inner = Mesh(mesh.devices.reshape(halves // 4, 4, 2, group // 2, 2), ALL)
    return jax.shard_map(
        shards,
        mesh=inner,
        in_specs=(P(ALL, None), P(ALL), P(ALL, None), P(ALL, None)),
        out_specs=(P(ALL), P(ALL)),
        check_vma=False,
    )
```

profile of v0, /device:TPU:2, one launch (start us, length us, event | category | flops | bytes accessed | tf_op | source)
XLA Modules:
  0.0 128.3 jit_solution(13958675157819855251)
XLA Ops:
  7.2 0.0 copy-start.5
  7.2 1.1 copy-done.5
  8.3 0.7 copy-done.6
  9.0 2.5 %shard_map.59 = (bf16[64,104,128]{2,1,0:T(8,128)(2,1)}, s32[2,512]{1,0:T(2,128)S(1)}) custom-call(bf16[512,768]{1,0:T(8,128)(2,1)S(1)} %copy-done.5, s32[1,512]{1,0:T(1,128)S(1)} %bitcast.20), custom_call_target="tpu_custom_call" | custom-call | flops 805306368 | bytes 2359296 | tf_op jit(solution)/shard_map/pallas_call | solution.py:83
  11.5 13.8 %all-to-all-start.1 = ((bf16[64,104,128]{2,1,0:T(8,128)(2,1)}), bf16[64,104,128]{2,1,0:T(8,128)(2,1)S(1)}, u32[]{:S(2)}, u32[]{:S(2)}) async-start(bf16[64,104,128]{2,1,0:T(8,128)(2,1)} %get-tuple-element.30), calls=%async_computation.1 | async-start | bytes 3407872 | tf_op jit(solution)/shard_map/all_to_all | solution.py:425
  25.3 0.0 all-gather.2.cloned.1.call-start
  25.4 0.0 copy-done.3
  25.4 0.9 shard_map.60
  26.3 0.0 all-gather.2.cloned.1.call-update
  26.3 5.7 %collective-permute-start.4 = (bf16[16,768]{1,0:T(8,128)(2,1)S(1)}, bf16[16,768]{1,0:T(8,128)(2,1)S(1)}, u32[]{:S(2)}, u32[]{:S(2)}) collective-permute-start(bf16[16,768]{1,0:T(8,128)(2,1)S(1)} %copy-done.4), channel_id=1, source_target_pairs={{0,128},{32,160},{64,192},{96,224},{128,0},{160,32},{192,64},{224,... | collective-permute-start | bytes 73736 | tf_op jit(solution)/shard_map/ppermute | solution.py:411
  32.0 0.5 collective-permute-start.3
  32.5 2.5 %collective-permute-start.5 = (bf16[16,768]{1,0:T(8,128)(2,1)S(1)}, bf16[16,768]{1,0:T(8,128)(2,1)S(1)}, u32[]{:S(2)}, u32[]{:S(2)}) collective-permute-start(bf16[16,768]{1,0:T(8,128)(2,1)S(1)} %copy-done.4), channel_id=1, source_target_pairs={{0,64},{32,96},{64,128},{96,160},{128,192},{160,224},{192,0},{224,... | collective-permute-start | bytes 73736 | tf_op jit(solution)/shard_map/ppermute | solution.py:411
  34.9 0.1 pad_add_fusion.where_ref
  35.0 34.1 %collective-permute-done.4.refs_2_ = bf16[16,768]{1,0:T(8,128)(2,1)S(1)} collective-permute-done((bf16[16,768]{1,0:T(8,128)(2,1)S(1)}, bf16[16,768]{1,0:T(8,128)(2,1)S(1)}, u32[]{:S(2)}, u32[]{:S(2)}) %collective-permute-start.4) | collective-permute-done | bytes 24608 | tf_op jit(solution)/shard_map/ppermute | solution.py:411
  69.2 0.0 collective-permute-done.3.refs_1_
  69.2 0.0 collective-permute-done.5.refs_3_
  69.2 0.1 collective-permute-start.10
  69.3 0.0 all-gather.2.cloned.1.call-done.refs_1_.refs_0_
  69.3 1.1 all-to-all-done.1.refs_0_
  70.4 2.9 %shard_map.63 = (bf16[400,768]{1,0:T(8,128)(2,1)S(1)}, bf16[400,768]{1,0:T(8,128)(2,1)S(1)}, f32[128,128]{1,0:T(8,128)S(1)}) custom-call(s32[4]{0:T(128)S(1)} %pad_add_fusion.where_ref, bf16[64,104,128]{2,1,0:T(8,128)(2,1)S(1)} %shard_map.62.own_ref), custom_call_target="tpu_custom_call" | custom-call | flops 1207959552 | bytes 2359296 | tf_op jit(solution)/shard_map/pallas_call | solution.py:283
  73.4 1.5 %collective-permute-start.6 = (bf16[400,768]{1,0:T(8,128)(2,1)S(1)}, bf16[400,768]{1,0:T(8,128)(2,1)S(1)}, u32[]{:S(2)}, u32[]{:S(2)}) collective-permute-start(bf16[400,768]{1,0:T(8,128)(2,1)S(1)} %get-tuple-element.32), channel_id=1, source_target_pairs={{0,1},{1,0},{2,3},{3,2},{4,5},{5,4},{6,7},{7,6},{8,9},{9,8},{10,11... | collective-permute-start | bytes 1843208 | tf_op jit(solution)/shard_map/ppermute | solution.py:429
  74.9 0.0 collective-permute-done.10.refs_1_
  74.9 2.5 %collective-permute-start.13 = (bf16[128,768]{1,0:T(8,128)(2,1)S(1)}, bf16[128,768]{1,0:T(8,128)(2,1)S(1)}, u32[]{:S(2)}, u32[]{:S(2)}) collective-permute-start(bf16[128,768]{1,0:T(8,128)(2,1)S(1)} %shard_map.65.refs_0_), channel_id=1, source_target_pairs={{0,16},{8,24},{16,0},{24,8},{1,17},{9,25},{17,1},{25,9},{2,18},{10... | collective-permute-start | bytes 589832 | tf_op jit(solution)/shard_map/ppermute | solution.py:436
  77.4 1.2 collective-permute-start.12
  78.5 0.9 collective-permute-start.11
  79.4 2.9 %collective-permute-done.13.refs_3_ = bf16[128,768]{1,0:T(8,128)(2,1)S(1)} collective-permute-done((bf16[128,768]{1,0:T(8,128)(2,1)S(1)}, bf16[128,768]{1,0:T(8,128)(2,1)S(1)}, u32[]{:S(2)}, u32[]{:S(2)}) %collective-permute-start.13) | collective-permute-done | bytes 196640 | tf_op jit(solution)/shard_map/ppermute | solution.py:436
  82.3 1.4 %collective-permute-done.12.refs_2_ = bf16[128,768]{1,0:T(8,128)(2,1)S(1)} collective-permute-done((bf16[128,768]{1,0:T(8,128)(2,1)S(1)}, bf16[128,768]{1,0:T(8,128)(2,1)S(1)}, u32[]{:S(2)}, u32[]{:S(2)}) %collective-permute-start.12) | collective-permute-done | bytes 196640 | tf_op jit(solution)/shard_map/ppermute | solution.py:435
  83.7 1.7 %collective-permute-done.11.refs_1_ = bf16[128,768]{1,0:T(8,128)(2,1)S(1)} collective-permute-done((bf16[128,768]{1,0:T(8,128)(2,1)S(1)}, bf16[128,768]{1,0:T(8,128)(2,1)S(1)}, u32[]{:S(2)}, u32[]{:S(2)}) %collective-permute-start.11) | collective-permute-done | bytes 196640 | tf_op jit(solution)/shard_map/ppermute | solution.py:434
  85.4 0.1 shard_map.66.mine_ref
  85.5 0.1 collective-permute-start.14
  85.6 0.5 collective-permute-start.7
  86.1 0.0 collective-permute-done.6.refs_1_
  86.1 0.1 collective-permute-start.8
  86.2 1.7 %collective-permute-done.14.other_ref = bf16[512,768]{1,0:T(8,128)(2,1)S(1)} collective-permute-done((bf16[512,768]{1,0:T(8,128)(2,1)S(1)}, bf16[512,768]{1,0:T(8,128)(2,1)S(1)}, u32[]{:S(2)}, u32[]{:S(2)}) %collective-permute-start.14) | collective-permute-done | bytes 786464 | tf_op jit(solution)/shard_map/ppermute | solution.py:438
  87.8 2.6 %shard_map.67 = (f32[64,16]{1,0:T(8,128)S(1)}, f32[64,16]{1,0:T(8,128)S(1)}) custom-call(s32[4]{0:T(128)S(1)} %pad_add_fusion.where_ref, bf16[512,768]{1,0:T(8,128)(2,1)S(1)} %shard_map.66.mine_ref, bf16[512,768]{1,0:T(8,128)(2,1)S(1)} %collective-permute-done.14.other_ref, bf16[1024,768]{1,0:T(8,128)(2,1)S(1)} %copy-done), custom_call_target="tpu_custom_call" | custom-call | flops 1610612736 | bytes 3145728 | tf_op jit(solution)/shard_map/pallas_call | solution.py:137
  90.4 0.2 collective-permute-start.15
  90.7 0.0 collective-permute-done.7.refs_2_
  90.7 0.0 collective-permute-done.8.refs_3_
  90.7 2.6 %shard_map.64 = (f32[1,512]{1,0:T(1,128)S(1)}, f32[1,512]{1,0:T(1,128)S(1)}) custom-call(bf16[400,768]{1,0:T(8,128)(2,1)S(1)} %get-tuple-element.31.refs_0_, bf16[400,768]{1,0:T(8,128)(2,1)S(1)} %collective-permute-done.6.refs_1_, bf16[400,768]{1,0:T(8,128)(2,1)S(1)} %collective-permute-done.7.refs_2_, bf16[400,768]{1,0:T(8,128)(2,1)S(1)} %collective-permute-done.8.refs_3_), custom_call_target="tpu_custom_call" | custom-call | flops 1811939328 | bytes 2359296 | tf_op jit(solution)/shard_map/pallas_call | solution.py:322
  93.3 1.2 collective-permute-start.9
  94.5 0.0 collective-permute-done.15.other_ref
  94.5 2.5 %collective-permute-done.9.back_ref = f32[1,512]{1,0:T(1,128)S(1)} collective-permute-done((f32[1,512]{1,0:T(1,128)S(1)}, f32[1,512]{1,0:T(1,128)S(1)}, u32[]{:S(2)}, u32[]{:S(2)}) %collective-permute-start.9) | collective-permute-done | bytes 2080 | tf_op jit(solution)/shard_map/ppermute | solution.py:446
  97.0 1.2 shard_map.68
  98.2 9.8 %all-to-all-start.2 = ((f32[64,1,48]{2,1,0:T(1,128)}), f32[64,1,48]{2,1,0:T(1,128)S(1)}, u32[]{:S(2)}, u32[]{:S(2)}) async-start(f32[64,1,48]{2,1,0:T(1,128)} %bitcast.10), calls=%async_computation.2 | async-start | bytes 65536 | tf_op jit(solution)/shard_map/all_to_all | solution.py:448
  108.1 12.0 %all-to-all-done.2 = f32[64,1,48]{2,1,0:T(1,128)S(1)} async-done(((f32[64,1,48]{2,1,0:T(1,128)}), f32[64,1,48]{2,1,0:T(1,128)S(1)}, u32[]{:S(2)}, u32[]{:S(2)}) %all-to-all-start.2) | async-done | bytes 12320 | tf_op jit(solution)/shard_map/all_to_all | solution.py:448
  120.0 0.8 shard_map.69
  120.8 0.0 copy-start.7
  120.9 0.6 copy-done.7
  (14 shorter events, 0.0 us)
Async XLA Ops:
  7.2 1.1 copy-start.5
  8.3 0.7 copy-start.6
  11.5 13.9 %copy-start.3 = (bf16[256,768]{1,0:T(8,128)(2,1)S(1)}, bf16[256,768]{1,0:T(8,128)(2,1)}, u32[]{:S(2)}) copy-start(bf16[256,768]{1,0:T(8,128)(2,1)} %in_ref.1) | copy-start | bytes 1179652
  11.5 14.8 %copy-start.4 = (bf16[16,768]{1,0:T(8,128)(2,1)S(1)}, bf16[16,768]{1,0:T(8,128)(2,1)}, u32[]{:S(2)}) copy-start(bf16[16,768]{1,0:T(8,128)(2,1)} %refs_0_.1) | copy-start | bytes 73732
  11.5 58.9 %all-to-all-start.1 = ((bf16[64,104,128]{2,1,0:T(8,128)(2,1)}), bf16[64,104,128]{2,1,0:T(8,128)(2,1)S(1)}, u32[]{:S(2)}, u32[]{:S(2)}) async-start(bf16[64,104,128]{2,1,0:T(8,128)(2,1)} %get-tuple-element.30), calls=%async_computation.1 | async-start | bytes 3407872 | tf_op jit(solution)/shard_map/all_to_all | solution.py:425
  25.3 44.0 %all-gather.2.cloned.1.call-start = ((), (), s32[]{:S(2)}) async-start(), calls=%async_computation.3 | async-start | bytes 1966080 | tf_op jit(solution)/shard_map/all_gather | solution.py:421
  26.3 42.8 %collective-permute-start.4 = (bf16[16,768]{1,0:T(8,128)(2,1)S(1)}, bf16[16,768]{1,0:T(8,128)(2,1)S(1)}, u32[]{:S(2)}, u32[]{:S(2)}) collective-permute-start(bf16[16,768]{1,0:T(8,128)(2,1)S(1)} %copy-done.4), channel_id=1, source_target_pairs={{0,128},{32,160},{64,192},{96,224},{128,0},{160,32},{192,64},{224,... | collective-permute-start | bytes 73736 | tf_op jit(solution)/shard_map/ppermute | solution.py:411
  32.0 37.1 %collective-permute-start.3 = (bf16[16,768]{1,0:T(8,128)(2,1)S(1)}, bf16[16,768]{1,0:T(8,128)(2,1)S(1)}, u32[]{:S(2)}, u32[]{:S(2)}) collective-permute-start(bf16[16,768]{1,0:T(8,128)(2,1)S(1)} %copy-done.4), channel_id=1, source_target_pairs={{0,192},{32,224},{64,0},{96,32},{128,64},{160,96},{192,128},{224,1... | collective-permute-start | bytes 73736 | tf_op jit(solution)/shard_map/ppermute | solution.py:411
  32.5 36.7 %collective-permute-start.5 = (bf16[16,768]{1,0:T(8,128)(2,1)S(1)}, bf16[16,768]{1,0:T(8,128)(2,1)S(1)}, u32[]{:S(2)}, u32[]{:S(2)}) collective-permute-start(bf16[16,768]{1,0:T(8,128)(2,1)S(1)} %copy-done.4), channel_id=1, source_target_pairs={{0,64},{32,96},{64,128},{96,160},{128,192},{160,224},{192,0},{224,... | collective-permute-start | bytes 73736 | tf_op jit(solution)/shard_map/ppermute | solution.py:411
  69.2 1.3 copy-start.1
  69.2 5.7 %collective-permute-start.10 = (bf16[64,768]{1,0:T(8,128)(2,1)S(1)}, bf16[64,768]{1,0:T(8,128)(2,1)S(1)}, u32[]{:S(2)}, u32[]{:S(2)}) collective-permute-start(bf16[64,768]{1,0:T(8,128)(2,1)S(1)} %shard_map.61.refs_2_.refs_0_), channel_id=1, source_target_pairs={{0,224},{32,0},{64,32},{96,64},{128,96},{160,128},{192,160},{224,1... | collective-permute-start | bytes 294920 | tf_op jit(solution)/shard_map/ppermute | solution.py:411
  70.4 4.4 %copy-start.2 = (bf16[64,768]{1,0:T(8,128)(2,1)S(1)}, bf16[64,768]{1,0:T(8,128)(2,1)}, u32[]{:S(2)}) copy-start(bf16[64,768]{1,0:T(8,128)(2,1)} %copy-done.1) | copy-start | bytes 294916
  73.3 14.5 %copy-start = (bf16[1024,768]{1,0:T(8,128)(2,1)S(1)}, bf16[1024,768]{1,0:T(8,128)(2,1)}, u32[]{:S(2)}) copy-start(bf16[1024,768]{1,0:T(8,128)(2,1)} %all-gather.2.cloned.1.call-done.refs_1_.refs_0_) | copy-start | bytes 4718596
  73.4 12.7 %collective-permute-start.6 = (bf16[400,768]{1,0:T(8,128)(2,1)S(1)}, bf16[400,768]{1,0:T(8,128)(2,1)S(1)}, u32[]{:S(2)}, u32[]{:S(2)}) collective-permute-start(bf16[400,768]{1,0:T(8,128)(2,1)S(1)} %get-tuple-element.32), channel_id=1, source_target_pairs={{0,1},{1,0},{2,3},{3,2},{4,5},{5,4},{6,7},{7,6},{8,9},{9,8},{10,11... | collective-permute-start | bytes 1843208 | tf_op jit(solution)/shard_map/ppermute | solution.py:429
  74.9 7.4 %collective-permute-start.13 = (bf16[128,768]{1,0:T(8,128)(2,1)S(1)}, bf16[128,768]{1,0:T(8,128)(2,1)S(1)}, u32[]{:S(2)}, u32[]{:S(2)}) collective-permute-start(bf16[128,768]{1,0:T(8,128)(2,1)S(1)} %shard_map.65.refs_0_), channel_id=1, source_target_pairs={{0,16},{8,24},{16,0},{24,8},{1,17},{9,25},{17,1},{25,9},{2,18},{10... | collective-permute-start | bytes 589832 | tf_op jit(solution)/shard_map/ppermute | solution.py:436
  77.4 6.3 %collective-permute-start.12 = (bf16[128,768]{1,0:T(8,128)(2,1)S(1)}, bf16[128,768]{1,0:T(8,128)(2,1)S(1)}, u32[]{:S(2)}, u32[]{:S(2)}) collective-permute-start(bf16[128,768]{1,0:T(8,128)(2,1)S(1)} %shard_map.65.refs_0_), channel_id=1, source_target_pairs={{0,24},{8,0},{16,8},{24,16},{1,25},{9,1},{17,9},{25,17},{2,26},{10... | collective-permute-start | bytes 589832 | tf_op jit(solution)/shard_map/ppermute | solution.py:435
  78.5 6.9 %collective-permute-start.11 = (bf16[128,768]{1,0:T(8,128)(2,1)S(1)}, bf16[128,768]{1,0:T(8,128)(2,1)S(1)}, u32[]{:S(2)}, u32[]{:S(2)}) collective-permute-start(bf16[128,768]{1,0:T(8,128)(2,1)S(1)} %shard_map.65.refs_0_), channel_id=1, source_target_pairs={{0,8},{8,16},{16,24},{24,0},{1,9},{9,17},{17,25},{25,1},{2,10},{10... | collective-permute-start | bytes 589832 | tf_op jit(solution)/shard_map/ppermute | solution.py:434
  85.5 2.4 %collective-permute-start.14 = (bf16[512,768]{1,0:T(8,128)(2,1)S(1)}, bf16[512,768]{1,0:T(8,128)(2,1)S(1)}, u32[]{:S(2)}, u32[]{:S(2)}) collective-permute-start(bf16[512,768]{1,0:T(8,128)(2,1)S(1)} %shard_map.66.mine_ref), channel_id=1, source_target_pairs={{0,4},{4,0},{1,5},{5,1},{2,6},{6,2},{3,7},{7,3},{8,12},{12,8},{9,1... | collective-permute-start | bytes 2359304 | tf_op jit(solution)/shard_map/ppermute | solution.py:438
  85.6 5.1 %collective-permute-start.7 = (bf16[400,768]{1,0:T(8,128)(2,1)S(1)}, bf16[400,768]{1,0:T(8,128)(2,1)S(1)}, u32[]{:S(2)}, u32[]{:S(2)}) collective-permute-start(bf16[400,768]{1,0:T(8,128)(2,1)S(1)} %get-tuple-element.31.refs_0_), channel_id=1, source_target_pairs={{0,4},{4,0},{1,5},{5,1},{2,6},{6,2},{3,7},{7,3},{8,12},{12,8},{9,1... | collective-permute-start | bytes 1843208 | tf_op jit(solution)/shard_map/ppermute | solution.py:430
  86.1 4.6 %collective-permute-start.8 = (bf16[400,768]{1,0:T(8,128)(2,1)S(1)}, bf16[400,768]{1,0:T(8,128)(2,1)S(1)}, u32[]{:S(2)}, u32[]{:S(2)}) collective-permute-start(bf16[400,768]{1,0:T(8,128)(2,1)S(1)} %collective-permute-done.6.refs_1_), channel_id=1, source_target_pairs={{0,4},{4,0},{1,5},{5,1},{2,6},{6,2},{3,7},{7,3},{8,12},{12,8},{9,1... | collective-permute-start | bytes 1843208 | tf_op jit(solution)/shard_map/ppermute | solution.py:444
  90.4 4.1 %collective-permute-start.15 = (f32[64,16]{1,0:T(8,128)S(1)}, f32[64,16]{1,0:T(8,128)S(1)}, u32[]{:S(2)}, u32[]{:S(2)}) collective-permute-start(f32[64,16]{1,0:T(8,128)S(1)} %get-tuple-element.37), channel_id=1, source_target_pairs={{0,4},{4,0},{1,5},{5,1},{2,6},{6,2},{3,7},{7,3},{8,12},{12,8},{9,1... | collective-permute-start | bytes 12296 | tf_op jit(solution)/shard_map/ppermute | solution.py:442
  93.3 3.7 %collective-permute-start.9 = (f32[1,512]{1,0:T(1,128)S(1)}, f32[1,512]{1,0:T(1,128)S(1)}, u32[]{:S(2)}, u32[]{:S(2)}) collective-permute-start(f32[1,512]{1,0:T(1,128)S(1)} %get-tuple-element.34), channel_id=1, source_target_pairs={{0,1},{1,0},{2,3},{3,2},{4,5},{5,4},{6,7},{7,6},{8,9},{9,8},{10,11... | collective-permute-start | bytes 6152 | tf_op jit(solution)/shard_map/ppermute | solution.py:446
  98.2 21.8 %all-to-all-start.2 = ((f32[64,1,48]{2,1,0:T(1,128)}), f32[64,1,48]{2,1,0:T(1,128)S(1)}, u32[]{:S(2)}, u32[]{:S(2)}) async-start(f32[64,1,48]{2,1,0:T(1,128)} %bitcast.10), calls=%async_computation.2 | async-start | bytes 65536 | tf_op jit(solution)/shard_map/all_to_all | solution.py:448
  120.8 0.6 copy-start.7
Sparse Core Ops, SparseCore 0:
  28.0 38.0 all-gather.1
where the time goes:
time: 129 us; the launch traced here: 128 us
  waiting for transfers between devices  57.5 us (45%)
  starting transfers between devices  40.5 us (31%)
  between operations  14.2 us (11%)
  Pallas kernels  13.6 us (11%)
  local copies, waits for them, and re-layouts  2.4 us (2%)
    ppermute x4, waiting for transfers between devices, moved(): lax.ppermute(block, axis, [(i, (i - by) % size) for i in range(size)])  34.2 us
    all_to_all x1, starting transfers between devices, shards(): landed = lax.all_to_all(send, OWN, split_axis=0, concat_axis=0, tiled=True)  13.8 us
    all_to_all x1, waiting for transfers between devices, shards(): back = lax.all_to_all(both, OWN, split_axis=0, concat_axis=0, tiled=True)  12 us
    all_to_all x1, starting transfers between devices, shards(): back = lax.all_to_all(both, OWN, split_axis=0, concat_axis=0, tiled=True)  9.82 us
    ppermute x4, starting transfers between devices, moved(): lax.ppermute(block, axis, [(i, (i - by) % size) for i in range(size)])  8.67 us
    pallas_call x1, Pallas kernels, split(): pl.pallas_call(functools.partial(split_kernel, cap, room), in_specs=[pl.B...  2.89 us
    ppermute x1, waiting for transfers between devices, shards(): far = lax.ppermute(line, 'y', [(i, (i + 2) % 4) for i in range(4)])  2.87 us
    pallas_call x1, Pallas kernels, list_best(): pl.pallas_call(functools.partial(list_kernel, room), out_shape=(jax.Shape...  2.65 us
  transfers between devices with their start and end apart: 16, of which 8 were waited for; matrix products, arithmetic and copies ran while one was open for 0% of the time, Pallas kernels for 7%

commit v1 on v0

--- a/solution.py
+++ b/solution.py
@@ -294,7 +294,7 @@
 
 
 def list_kernel(room, *refs):
-    list_refs, (keep_ref, came_ref) = refs[:4], refs[4:]
+    list_refs, out_ref = refs[:4], refs[4]
     over = jnp.zeros((1, 1), F32)
     counts = []
     for ref in list_refs:
@@ -304,26 +304,25 @@
     other = lax.broadcasted_iota(jnp.int32, (room, room), 0)
     mine = lax.broadcasted_iota(jnp.int32, (room, room), 1)
     position = lax.broadcasted_iota(jnp.int32, (room, 1), 0).astype(F32)
-    for k, out_ref in ((0, keep_ref), (1, came_ref)):
-        own = list_refs[k][:room, :]
-        best = jnp.full((1, room), -1.0, F32)
-        for j, ref in enumerate(list_refs):
-            scores = dot_t(ref[:room, :], own)
-            use = position < counts[j]
-            if j == k:
-                use = use & (other != mine)
-            best = jnp.maximum(best, jnp.max(jnp.where(use, scores, -1.0), axis=0, keepdims=True))
-        out_ref[:, :room] = best
-        out_ref[:, room:] = jnp.broadcast_to(over, (1, 128))
+    own = list_refs[0][:room, :]
+    best = jnp.full((1, room), -1.0, F32)
+    for j, ref in enumerate(list_refs):
+        scores = dot_t(ref[:room, :], own)
+        use = position < counts[j]
+        if j == 0:
+            use = use & (other != mine)
+        best = jnp.maximum(best, jnp.max(jnp.where(use, scores, -1.0), axis=0, keepdims=True))
+    out_ref[:, :room] = best
+    out_ref[:, room:] = jnp.broadcast_to(over, (1, 128))
 
 
 def list_best(lists, room):
     width = lists[0].shape[1]
     return pl.pallas_call(
         functools.partial(list_kernel, room),
-        out_shape=(jax.ShapeDtypeStruct((1, room + 128), F32),) * 2,
-        compiler_params=params(),
-        cost_estimate=cost(16 * room * room * width, 8 * room * width),
+        out_shape=jax.ShapeDtypeStruct((1, room + 128), F32),
+        compiler_params=params(),
+        cost_estimate=cost(8 * room * room * width, 8 * room * width),
     )(*lists)
 
 
@@ -442,8 +441,8 @@
     cent_back = lax.ppermute(cent_theirs, "c", SWAP)
 
     came_c = lax.ppermute(came, "c", SWAP)
-    kept, guests = list_best([keep, came, keep_c, came_c], room)
-    guests = lax.ppermute(guests, "xl", SWAP)
+    guests = lax.ppermute(list_best([came, keep, keep_c, came_c], room), "xl", SWAP)
+    kept = list_best([keep, came, keep_c, came_c], room)
     both = merge(kept, guests, spots, cent_mine, cent_back, room)
     back = lax.all_to_all(both, OWN, split_axis=0, concat_axis=0, tiled=True)
     dup, cent_score, over = unpack(back, place, owners, cap)

time: 129 us -> 127 us (0.984)
  waiting for transfers between devices: 57.5 us -> 56.1 us
    ppermute x1, waiting for transfers between devices: 2.51 us -> 1.1 us  [shards(): lax.ppermute(list_best([came, keep, keep_c, came_c], room), 'xl', SWAP)]
    pallas_call x1 -> x2, Pallas kernels: 2.65 us -> 2.82 us  [list_best(): pl.pallas_call(functools.partial(list_kernel, room), out_shape=jax.ShapeD...]
where the time goes in v1:
time: 127 us
  waiting for transfers between devices  56.1 us (44%)
  starting transfers between devices  40.4 us (32%)
  between operations  14.2 us (11%)
  Pallas kernels  13.8 us (11%)
  local copies, waits for them, and re-layouts  2.4 us (2%)
    ppermute x4, waiting for transfers between devices, moved(): lax.ppermute(block, axis, [(i, (i - by) % size) for i in range(size)])  34.2 us
    all_to_all x1, starting transfers between devices, shards(): landed = lax.all_to_all(send, OWN, split_axis=0, concat_axis=0, tiled=True)  13.8 us
    all_to_all x1, waiting for transfers between devices, shards(): back = lax.all_to_all(both, OWN, split_axis=0, concat_axis=0, tiled=True)  12 us
    all_to_all x1, starting transfers between devices, shards(): back = lax.all_to_all(both, OWN, split_axis=0, concat_axis=0, tiled=True)  9.83 us
    ppermute x4, starting transfers between devices, moved(): lax.ppermute(block, axis, [(i, (i - by) % size) for i in range(size)])  8.67 us
    pallas_call x1, Pallas kernels, split(): pl.pallas_call(functools.partial(split_kernel, cap, room), in_specs=[pl.B...  2.9 us
    ppermute x1, waiting for transfers between devices, shards(): far = lax.ppermute(line, 'y', [(i, (i + 2) % 4) for i in range(4)])  2.86 us
    pallas_call x2, Pallas kernels, list_best(): pl.pallas_call(functools.partial(list_kernel, room), out_shape=jax.ShapeD...  2.82 us
  transfers between devices with their start and end apart: 16, of which 8 were waited for; matrix products, arithmetic and copies ran while one was open for 0% of the time, Pallas kernels for 7%

profile of v1, /device:TPU:2, one launch (start us, length us, event | category | flops | bytes accessed | tf_op | source)
XLA Modules:
  0.0 127.1 jit_solution(9763867201942159443)
XLA Ops:
  7.2 1.1 copy-done.5
  8.3 0.7 copy-done.6
  9.0 2.5 %shard_map.59 = (bf16[64,104,128]{2,1,0:T(8,128)(2,1)}, s32[2,512]{1,0:T(2,128)S(1)}) custom-call(bf16[512,768]{1,0:T(8,128)(2,1)S(1)} %copy-done.5, s32[1,512]{1,0:T(1,128)S(1)} %bitcast.20), custom_call_target="tpu_custom_call" | custom-call | flops 805306368 | bytes 2359296 | tf_op jit(solution)/shard_map/pallas_call | solution.py:83
  11.5 13.8 %all-to-all-start.1 = ((bf16[64,104,128]{2,1,0:T(8,128)(2,1)}), bf16[64,104,128]{2,1,0:T(8,128)(2,1)S(1)}, u32[]{:S(2)}, u32[]{:S(2)}) async-start(bf16[64,104,128]{2,1,0:T(8,128)(2,1)} %get-tuple-element.28), calls=%async_computation.1 | async-start | bytes 3407872 | tf_op jit(solution)/shard_map/all_to_all | solution.py:424
  25.3 0.0 all-gather.2.cloned.1.call-start
  25.4 0.9 shard_map.60
  26.3 0.0 all-gather.2.cloned.1.call-update
  26.3 5.7 %collective-permute-start.4 = (bf16[16,768]{1,0:T(8,128)(2,1)S(1)}, bf16[16,768]{1,0:T(8,128)(2,1)S(1)}, u32[]{:S(2)}, u32[]{:S(2)}) collective-permute-start(bf16[16,768]{1,0:T(8,128)(2,1)S(1)} %copy-done.4), channel_id=1, source_target_pairs={{0,128},{32,160},{64,192},{96,224},{128,0},{160,32},{192,64},{224,... | collective-permute-start | bytes 73736 | tf_op jit(solution)/shard_map/ppermute | solution.py:410
  32.0 0.5 collective-permute-start.3
  32.5 2.5 %collective-permute-start.5 = (bf16[16,768]{1,0:T(8,128)(2,1)S(1)}, bf16[16,768]{1,0:T(8,128)(2,1)S(1)}, u32[]{:S(2)}, u32[]{:S(2)}) collective-permute-start(bf16[16,768]{1,0:T(8,128)(2,1)S(1)} %copy-done.4), channel_id=1, source_target_pairs={{0,64},{32,96},{64,128},{96,160},{128,192},{160,224},{192,0},{224,... | collective-permute-start | bytes 73736 | tf_op jit(solution)/shard_map/ppermute | solution.py:410
  34.9 0.1 pad_add_fusion.where_ref
  35.0 34.2 %collective-permute-done.4.refs_2_ = bf16[16,768]{1,0:T(8,128)(2,1)S(1)} collective-permute-done((bf16[16,768]{1,0:T(8,128)(2,1)S(1)}, bf16[16,768]{1,0:T(8,128)(2,1)S(1)}, u32[]{:S(2)}, u32[]{:S(2)}) %collective-permute-start.4) | collective-permute-done | bytes 24608 | tf_op jit(solution)/shard_map/ppermute | solution.py:410
  69.2 0.0 collective-permute-done.3.refs_1_
  69.2 0.0 collective-permute-done.5.refs_3_
  69.2 0.1 collective-permute-start.10
  69.3 0.0 all-gather.2.cloned.1.call-done.refs_1_.refs_0_
  69.3 1.1 all-to-all-done.1.refs_0_
  70.4 2.9 %shard_map.63 = (bf16[400,768]{1,0:T(8,128)(2,1)S(1)}, bf16[400,768]{1,0:T(8,128)(2,1)S(1)}, f32[128,128]{1,0:T(8,128)S(1)}) custom-call(s32[4]{0:T(128)S(1)} %pad_add_fusion.where_ref, bf16[64,104,128]{2,1,0:T(8,128)(2,1)S(1)} %shard_map.62.own_ref), custom_call_target="tpu_custom_call" | custom-call | flops 1207959552 | bytes 2359296 | tf_op jit(solution)/shard_map/pallas_call | solution.py:283
  73.4 1.5 %collective-permute-start.6 = (bf16[400,768]{1,0:T(8,128)(2,1)S(1)}, bf16[400,768]{1,0:T(8,128)(2,1)S(1)}, u32[]{:S(2)}, u32[]{:S(2)}) collective-permute-start(bf16[400,768]{1,0:T(8,128)(2,1)S(1)} %get-tuple-element.30), channel_id=1, source_target_pairs={{0,1},{1,0},{2,3},{3,2},{4,5},{5,4},{6,7},{7,6},{8,9},{9,8},{10,11... | collective-permute-start | bytes 1843208 | tf_op jit(solution)/shard_map/ppermute | solution.py:428
  74.9 0.0 collective-permute-done.10.refs_1_
  74.9 0.0 copy-done.2
  74.9 2.5 %collective-permute-start.13 = (bf16[128,768]{1,0:T(8,128)(2,1)S(1)}, bf16[128,768]{1,0:T(8,128)(2,1)S(1)}, u32[]{:S(2)}, u32[]{:S(2)}) collective-permute-start(bf16[128,768]{1,0:T(8,128)(2,1)S(1)} %shard_map.66.refs_0_), channel_id=1, source_target_pairs={{0,16},{8,24},{16,0},{24,8},{1,17},{9,25},{17,1},{25,9},{2,18},{10... | collective-permute-start | bytes 589832 | tf_op jit(solution)/shard_map/ppermute | solution.py:435
  77.4 1.2 collective-permute-start.12
  78.5 0.9 collective-permute-start.11
  79.4 2.9 %collective-permute-done.13.refs_3_ = bf16[128,768]{1,0:T(8,128)(2,1)S(1)} collective-permute-done((bf16[128,768]{1,0:T(8,128)(2,1)S(1)}, bf16[128,768]{1,0:T(8,128)(2,1)S(1)}, u32[]{:S(2)}, u32[]{:S(2)}) %collective-permute-start.13) | collective-permute-done | bytes 196640 | tf_op jit(solution)/shard_map/ppermute | solution.py:435
  82.3 1.4 %collective-permute-done.12.refs_2_ = bf16[128,768]{1,0:T(8,128)(2,1)S(1)} collective-permute-done((bf16[128,768]{1,0:T(8,128)(2,1)S(1)}, bf16[128,768]{1,0:T(8,128)(2,1)S(1)}, u32[]{:S(2)}, u32[]{:S(2)}) %collective-permute-start.12) | collective-permute-done | bytes 196640 | tf_op jit(solution)/shard_map/ppermute | solution.py:434
  83.7 1.7 %collective-permute-done.11.refs_1_ = bf16[128,768]{1,0:T(8,128)(2,1)S(1)} collective-permute-done((bf16[128,768]{1,0:T(8,128)(2,1)S(1)}, bf16[128,768]{1,0:T(8,128)(2,1)S(1)}, u32[]{:S(2)}, u32[]{:S(2)}) %collective-permute-start.11) | collective-permute-done | bytes 196640 | tf_op jit(solution)/shard_map/ppermute | solution.py:433
  85.4 0.1 shard_map.67.mine_ref
  85.5 0.1 collective-permute-start.14
  85.6 0.5 collective-permute-start.7
  86.1 0.0 collective-permute-done.6.refs_1_.refs_0_
  86.1 0.1 collective-permute-start.8
  86.2 1.7 %collective-permute-done.14.other_ref = bf16[512,768]{1,0:T(8,128)(2,1)S(1)} collective-permute-done((bf16[512,768]{1,0:T(8,128)(2,1)S(1)}, bf16[512,768]{1,0:T(8,128)(2,1)S(1)}, u32[]{:S(2)}, u32[]{:S(2)}) %collective-permute-start.14) | collective-permute-done | bytes 786464 | tf_op jit(solution)/shard_map/ppermute | solution.py:437
  87.9 2.6 %shard_map.68 = (f32[64,16]{1,0:T(8,128)S(1)}, f32[64,16]{1,0:T(8,128)S(1)}) custom-call(s32[4]{0:T(128)S(1)} %pad_add_fusion.where_ref, bf16[512,768]{1,0:T(8,128)(2,1)S(1)} %shard_map.67.mine_ref, bf16[512,768]{1,0:T(8,128)(2,1)S(1)} %collective-permute-done.14.other_ref, bf16[1024,768]{1,0:T(8,128)(2,1)S(1)} %copy-done), custom_call_target="tpu_custom_call" | custom-call | flops 1610612736 | bytes 3145728 | tf_op jit(solution)/shard_map/pallas_call | solution.py:137
  90.4 0.2 collective-permute-start.15
  90.7 0.0 collective-permute-done.7.refs_2_
  90.7 0.0 collective-permute-done.8.refs_3_
  90.7 1.4 %shard_map.65 = f32[1,512]{1,0:T(1,128)S(1)} custom-call(bf16[400,768]{1,0:T(8,128)(2,1)S(1)} %collective-permute-done.6.refs_1_.refs_0_, bf16[400,768]{1,0:T(8,128)(2,1)S(1)} %get-tuple-element.29.refs_0_.refs_1_, bf16[400,768]{1,0:T(8,128)(2,1)S(1)} %collective-permute-done.7.refs_2_, bf16[400,768]{1,0:T(8,128)(2,1)S(1)} %collective-permute-done.8.refs_3_), custom_call_target="tpu_custom_call" | custom-call | flops 905969664 | bytes 2359296 | tf_op jit(solution)/shard_map/pallas_call | solution.py:321
  92.1 1.2 collective-permute-start.9
  93.2 1.4 %shard_map.64.kept_ref = f32[1,512]{1,0:T(1,128)S(1)} custom-call(bf16[400,768]{1,0:T(8,128)(2,1)S(1)} %get-tuple-element.29.refs_0_.refs_1_, bf16[400,768]{1,0:T(8,128)(2,1)S(1)} %collective-permute-done.6.refs_1_.refs_0_, bf16[400,768]{1,0:T(8,128)(2,1)S(1)} %collective-permute-done.7.refs_2_, bf16[400,768]{1,0:T(8,128)(2,1)S(1)} %collective-permute-done.8.refs_3_), custom_call_target="tpu_custom_call" | custom-call | flops 905969664 | bytes 2359296 | tf_op jit(solution)/shard_map/pallas_call | solution.py:321
  94.7 0.0 collective-permute-done.15.other_ref
  94.7 1.1 collective-permute-done.9.back_ref
  95.8 1.2 shard_map.69
  97.0 9.8 %all-to-all-start.2 = ((f32[64,1,48]{2,1,0:T(1,128)}), f32[64,1,48]{2,1,0:T(1,128)S(1)}, u32[]{:S(2)}, u32[]{:S(2)}) async-start(f32[64,1,48]{2,1,0:T(1,128)} %bitcast.10), calls=%async_computation.2 | async-start | bytes 65536 | tf_op jit(solution)/shard_map/all_to_all | solution.py:447
  106.9 12.0 %all-to-all-done.2 = f32[64,1,48]{2,1,0:T(1,128)S(1)} async-done(((f32[64,1,48]{2,1,0:T(1,128)}), f32[64,1,48]{2,1,0:T(1,128)S(1)}, u32[]{:S(2)}, u32[]{:S(2)}) %all-to-all-start.2) | async-done | bytes 12320 | tf_op jit(solution)/shard_map/all_to_all | solution.py:447
  118.8 0.8 shard_map.70
  119.6 0.0 copy-start.7
  119.6 0.6 copy-done.7
  (15 shorter events, 0.0 us)
Async XLA Ops:
  7.2 1.1 copy-start.5
  8.3 0.7 copy-start.6
  11.5 13.9 %copy-start.3 = (bf16[256,768]{1,0:T(8,128)(2,1)S(1)}, bf16[256,768]{1,0:T(8,128)(2,1)}, u32[]{:S(2)}) copy-start(bf16[256,768]{1,0:T(8,128)(2,1)} %in_ref.1) | copy-start | bytes 1179652
  11.5 14.8 %copy-start.4 = (bf16[16,768]{1,0:T(8,128)(2,1)S(1)}, bf16[16,768]{1,0:T(8,128)(2,1)}, u32[]{:S(2)}) copy-start(bf16[16,768]{1,0:T(8,128)(2,1)} %refs_0_.1) | copy-start | bytes 73732
  11.5 58.9 %all-to-all-start.1 = ((bf16[64,104,128]{2,1,0:T(8,128)(2,1)}), bf16[64,104,128]{2,1,0:T(8,128)(2,1)S(1)}, u32[]{:S(2)}, u32[]{:S(2)}) async-start(bf16[64,104,128]{2,1,0:T(8,128)(2,1)} %get-tuple-element.28), calls=%async_computation.1 | async-start | bytes 3407872 | tf_op jit(solution)/shard_map/all_to_all | solution.py:424
  25.3 44.0 %all-gather.2.cloned.1.call-start = ((), (), s32[]{:S(2)}) async-start(), calls=%async_computation.3 | async-start | bytes 1966080 | tf_op jit(solution)/shard_map/all_gather | solution.py:420
  26.3 42.8 %collective-permute-start.4 = (bf16[16,768]{1,0:T(8,128)(2,1)S(1)}, bf16[16,768]{1,0:T(8,128)(2,1)S(1)}, u32[]{:S(2)}, u32[]{:S(2)}) collective-permute-start(bf16[16,768]{1,0:T(8,128)(2,1)S(1)} %copy-done.4), channel_id=1, source_target_pairs={{0,128},{32,160},{64,192},{96,224},{128,0},{160,32},{192,64},{224,... | collective-permute-start | bytes 73736 | tf_op jit(solution)/shard_map/ppermute | solution.py:410
  32.0 37.2 %collective-permute-start.3 = (bf16[16,768]{1,0:T(8,128)(2,1)S(1)}, bf16[16,768]{1,0:T(8,128)(2,1)S(1)}, u32[]{:S(2)}, u32[]{:S(2)}) collective-permute-start(bf16[16,768]{1,0:T(8,128)(2,1)S(1)} %copy-done.4), channel_id=1, source_target_pairs={{0,192},{32,224},{64,0},{96,32},{128,64},{160,96},{192,128},{224,1... | collective-permute-start | bytes 73736 | tf_op jit(solution)/shard_map/ppermute | solution.py:410
  32.5 36.7 %collective-permute-start.5 = (bf16[16,768]{1,0:T(8,128)(2,1)S(1)}, bf16[16,768]{1,0:T(8,128)(2,1)S(1)}, u32[]{:S(2)}, u32[]{:S(2)}) collective-permute-start(bf16[16,768]{1,0:T(8,128)(2,1)S(1)} %copy-done.4), channel_id=1, source_target_pairs={{0,64},{32,96},{64,128},{96,160},{128,192},{160,224},{192,0},{224,... | collective-permute-start | bytes 73736 | tf_op jit(solution)/shard_map/ppermute | solution.py:410
  69.2 1.3 copy-start.1
  69.2 5.7 %collective-permute-start.10 = (bf16[64,768]{1,0:T(8,128)(2,1)S(1)}, bf16[64,768]{1,0:T(8,128)(2,1)S(1)}, u32[]{:S(2)}, u32[]{:S(2)}) collective-permute-start(bf16[64,768]{1,0:T(8,128)(2,1)S(1)} %shard_map.61.refs_2_.refs_0_), channel_id=1, source_target_pairs={{0,224},{32,0},{64,32},{96,64},{128,96},{160,128},{192,160},{224,1... | collective-permute-start | bytes 294920 | tf_op jit(solution)/shard_map/ppermute | solution.py:410
  70.4 4.4 %copy-start.2 = (bf16[64,768]{1,0:T(8,128)(2,1)S(1)}, bf16[64,768]{1,0:T(8,128)(2,1)}, u32[]{:S(2)}) copy-start(bf16[64,768]{1,0:T(8,128)(2,1)} %copy-done.1) | copy-start | bytes 294916
  73.3 14.5 %copy-start = (bf16[1024,768]{1,0:T(8,128)(2,1)S(1)}, bf16[1024,768]{1,0:T(8,128)(2,1)}, u32[]{:S(2)}) copy-start(bf16[1024,768]{1,0:T(8,128)(2,1)} %all-gather.2.cloned.1.call-done.refs_1_.refs_0_) | copy-start | bytes 4718596
  73.4 12.7 %collective-permute-start.6 = (bf16[400,768]{1,0:T(8,128)(2,1)S(1)}, bf16[400,768]{1,0:T(8,128)(2,1)S(1)}, u32[]{:S(2)}, u32[]{:S(2)}) collective-permute-start(bf16[400,768]{1,0:T(8,128)(2,1)S(1)} %get-tuple-element.30), channel_id=1, source_target_pairs={{0,1},{1,0},{2,3},{3,2},{4,5},{5,4},{6,7},{7,6},{8,9},{9,8},{10,11... | collective-permute-start | bytes 1843208 | tf_op jit(solution)/shard_map/ppermute | solution.py:428
  74.9 7.4 %collective-permute-start.13 = (bf16[128,768]{1,0:T(8,128)(2,1)S(1)}, bf16[128,768]{1,0:T(8,128)(2,1)S(1)}, u32[]{:S(2)}, u32[]{:S(2)}) collective-permute-start(bf16[128,768]{1,0:T(8,128)(2,1)S(1)} %shard_map.66.refs_0_), channel_id=1, source_target_pairs={{0,16},{8,24},{16,0},{24,8},{1,17},{9,25},{17,1},{25,9},{2,18},{10... | collective-permute-start | bytes 589832 | tf_op jit(solution)/shard_map/ppermute | solution.py:435
  77.4 6.3 %collective-permute-start.12 = (bf16[128,768]{1,0:T(8,128)(2,1)S(1)}, bf16[128,768]{1,0:T(8,128)(2,1)S(1)}, u32[]{:S(2)}, u32[]{:S(2)}) collective-permute-start(bf16[128,768]{1,0:T(8,128)(2,1)S(1)} %shard_map.66.refs_0_), channel_id=1, source_target_pairs={{0,24},{8,0},{16,8},{24,16},{1,25},{9,1},{17,9},{25,17},{2,26},{10... | collective-permute-start | bytes 589832 | tf_op jit(solution)/shard_map/ppermute | solution.py:434
  78.5 6.9 %collective-permute-start.11 = (bf16[128,768]{1,0:T(8,128)(2,1)S(1)}, bf16[128,768]{1,0:T(8,128)(2,1)S(1)}, u32[]{:S(2)}, u32[]{:S(2)}) collective-permute-start(bf16[128,768]{1,0:T(8,128)(2,1)S(1)} %shard_map.66.refs_0_), channel_id=1, source_target_pairs={{0,8},{8,16},{16,24},{24,0},{1,9},{9,17},{17,25},{25,1},{2,10},{10... | collective-permute-start | bytes 589832 | tf_op jit(solution)/shard_map/ppermute | solution.py:433
  85.5 2.4 %collective-permute-start.14 = (bf16[512,768]{1,0:T(8,128)(2,1)S(1)}, bf16[512,768]{1,0:T(8,128)(2,1)S(1)}, u32[]{:S(2)}, u32[]{:S(2)}) collective-permute-start(bf16[512,768]{1,0:T(8,128)(2,1)S(1)} %shard_map.67.mine_ref), channel_id=1, source_target_pairs={{0,4},{4,0},{1,5},{5,1},{2,6},{6,2},{3,7},{7,3},{8,12},{12,8},{9,1... | collective-permute-start | bytes 2359304 | tf_op jit(solution)/shard_map/ppermute | solution.py:437
  85.6 5.1 %collective-permute-start.7 = (bf16[400,768]{1,0:T(8,128)(2,1)S(1)}, bf16[400,768]{1,0:T(8,128)(2,1)S(1)}, u32[]{:S(2)}, u32[]{:S(2)}) collective-permute-start(bf16[400,768]{1,0:T(8,128)(2,1)S(1)} %get-tuple-element.29.refs_0_.refs_1_), channel_id=1, source_target_pairs={{0,4},{4,0},{1,5},{5,1},{2,6},{6,2},{3,7},{7,3},{8,12},{12,8},{9,1... | collective-permute-start | bytes 1843208 | tf_op jit(solution)/shard_map/ppermute | solution.py:429
  86.1 4.6 %collective-permute-start.8 = (bf16[400,768]{1,0:T(8,128)(2,1)S(1)}, bf16[400,768]{1,0:T(8,128)(2,1)S(1)}, u32[]{:S(2)}, u32[]{:S(2)}) collective-permute-start(bf16[400,768]{1,0:T(8,128)(2,1)S(1)} %collective-permute-done.6.refs_1_.refs_0_), channel_id=1, source_target_pairs={{0,4},{4,0},{1,5},{5,1},{2,6},{6,2},{3,7},{7,3},{8,12},{12,8},{9,1... | collective-permute-start | bytes 1843208 | tf_op jit(solution)/shard_map/ppermute | solution.py:443
  90.4 4.2 %collective-permute-start.15 = (f32[64,16]{1,0:T(8,128)S(1)}, f32[64,16]{1,0:T(8,128)S(1)}, u32[]{:S(2)}, u32[]{:S(2)}) collective-permute-start(f32[64,16]{1,0:T(8,128)S(1)} %get-tuple-element.33), channel_id=1, source_target_pairs={{0,4},{4,0},{1,5},{5,1},{2,6},{6,2},{3,7},{7,3},{8,12},{12,8},{9,1... | collective-permute-start | bytes 12296 | tf_op jit(solution)/shard_map/ppermute | solution.py:441
  92.1 3.7 %collective-permute-start.9 = (f32[1,512]{1,0:T(1,128)S(1)}, f32[1,512]{1,0:T(1,128)S(1)}, u32[]{:S(2)}, u32[]{:S(2)}) collective-permute-start(f32[1,512]{1,0:T(1,128)S(1)} %shard_map.65), channel_id=1, source_target_pairs={{0,1},{1,0},{2,3},{3,2},{4,5},{5,4},{6,7},{7,6},{8,9},{9,8},{10,11... | collective-permute-start | bytes 6152 | tf_op jit(solution)/shard_map/ppermute | solution.py:444
  97.0 21.8 %all-to-all-start.2 = ((f32[64,1,48]{2,1,0:T(1,128)}), f32[64,1,48]{2,1,0:T(1,128)S(1)}, u32[]{:S(2)}, u32[]{:S(2)}) async-start(f32[64,1,48]{2,1,0:T(1,128)} %bitcast.10), calls=%async_computation.2 | async-start | bytes 65536 | tf_op jit(solution)/shard_map/all_to_all | solution.py:447
  119.6 0.6 copy-start.7
Sparse Core Ops, SparseCore 0:
  28.0 38.0 all-gather.1
